TPU v7x, 32 devices: a whole 2x2x4 slice. The times are simulated.
32 devices in a mesh: dp: 4 (over z), shard: 8 (over y, x, core).
Axes of the slice: x: 2, y: 2, z: 4, core: 2. Of those that a mesh axis runs over, the one named last changes fastest.
Arguments:
- grads: bfloat16 [4, 16, 256, 256], P('dp', None, 'shard'), may hold values from -24 to 24
- owner_table: int32 [4, 16], replicated, may hold values from 0 to 3, as said below
- block_counts: int32 [4, 8], replicated, may hold values from 0 to 2, as said below
- prev_left: float32 [64, 256, 256], P(('dp', 'shard')), as said below
- prev_right: float32 [64, 256, 256], P(('dp', 'shard')), as said below
Outputs:
- updates: bfloat16 [16, 256, 256], P(None, 'shard')
Inputs may be any that keep to these rules, and one draw needn't show every extreme that they name: `owner_table`: for group d and owner o, entries o * 2 to o * 2 + block_counts[d, o] - 1 of row d name blocks of the group, and these live entries together name each of the group's 4 blocks exactly once; the other entries name arbitrary blocks of the group. `block_counts`: each row sums to 4; in every row some owner has exactly 2 blocks. `prev_left`: each slot's matrix is symmetric positive semidefinite. `prev_right`: each slot's matrix is symmetric positive semidefinite.
All inputs are finite; a program needn't handle non-finite values.
Results may differ from a plain program's by a relative error of at most 0.02.
Values may be sent and summed in bfloat16 or wider, within the bound.
A program may use at most 64 MiB of HBM per device.

v0:
```python
import jax
import jax.numpy as jnp
from jax import lax
from jax.sharding import PartitionSpec as P

CAP = 2


stat_decay = 0.9
eps_small = 1e-06


def inverse_root(factor):
    size_now = factor.shape[0]
    unit_matrix = jnp.eye(size_now, dtype=jnp.float32)
    norm_scale = size_now * jnp.sqrt(jnp.mean(factor * factor) + eps_small)
    start = factor / norm_scale
    first = (1.25 * unit_matrix - 0.25 * start).astype(jnp.bfloat16)
    square = jnp.dot(first, first, preferred_element_type=jnp.float32).astype(jnp.bfloat16)
    fourth = jnp.dot(square, square, preferred_element_type=jnp.float32).astype(jnp.bfloat16)
    next_state = jnp.dot(fourth, start.astype(jnp.bfloat16), preferred_element_type=jnp.float32)
    second = (1.25 * unit_matrix - 0.25 * next_state).astype(jnp.bfloat16)
    return jnp.dot(first, second, preferred_element_type=jnp.float32).astype(jnp.bfloat16)


def precondition(grad_block, left_prev, right_prev):
    left_factor = stat_decay * left_prev + (1.0 - stat_decay) * jnp.dot(
        grad_block, grad_block.T, preferred_element_type=jnp.float32
    )
    right_factor = stat_decay * right_prev + (1.0 - stat_decay) * jnp.dot(
        grad_block.T, grad_block, preferred_element_type=jnp.float32
    )
    root_left = inverse_root(left_factor)
    root_right = inverse_root(right_factor)
    half_done = jnp.dot(root_left, grad_block, preferred_element_type=jnp.float32).astype(
        jnp.bfloat16
    )
    precond = jnp.dot(half_done, root_right, preferred_element_type=jnp.float32)
    grad_wide = grad_block.astype(jnp.float32)
    grad_norm = jnp.sqrt(jnp.mean(grad_wide * grad_wide) + eps_small)
    cond_norm = jnp.sqrt(jnp.mean(precond * precond) + eps_small)
    return (precond * (grad_norm / cond_norm)).astype(jnp.bfloat16)


def refresh(arrived, prev_left, prev_right):
    return jax.vmap(precondition)(arrived, prev_left, prev_right)


def body(grads, owner_table, block_counts, prev_left, prev_right):
    owners = lax.axis_size("shard")
    groups = lax.axis_size("dp")
    my_group = lax.axis_index("dp")
    blocks = grads.shape[1]
    row_count = grads.shape[2]
    block_width = grads.shape[3]
    per_group = blocks // groups
    slot_total = owners * CAP
    slot_ids = jnp.arange(slot_total, dtype=jnp.int32)
    is_live = (slot_ids % CAP)[None, :] < block_counts[:, slot_ids // CAP]
    matches = (
        owner_table[:, None, :] == jnp.arange(per_group, dtype=jnp.int32)[None, :, None]
    ) & is_live[:, None, :]
    earliest = jnp.min(jnp.where(matches, slot_ids[None, None, :], slot_total), axis=2)
    has_slot = earliest < slot_total
    earliest = jnp.minimum(earliest, slot_total - 1)
    pick_index = earliest % CAP * owners + earliest // CAP
    local_terms = grads[0].astype(jnp.float32)
    summed = lax.psum_scatter(
        local_terms.astype(jnp.bfloat16), "dp", scatter_dimension=0, tiled=True
    )
    table_row = owner_table[my_group].reshape(owners, CAP).T
    outgoing = jnp.take(summed, table_row, axis=0)
    arrived = lax.all_to_all(outgoing, "shard", split_axis=1, concat_axis=1, tiled=True).reshape(
        CAP, block_width, block_width
    )
    fresh = refresh(arrived, prev_left, prev_right)
    returned = lax.all_to_all(
        fresh.reshape(CAP, owners, row_count, block_width),
        "shard",
        split_axis=1,
        concat_axis=1,
        tiled=True,
    )
    chosen = jnp.take(
        returned.reshape(CAP * owners, row_count, block_width), pick_index[my_group], axis=0
    )
    chosen = jnp.where(has_slot[my_group][:, None, None], chosen, jnp.zeros_like(chosen))
    return lax.all_gather(chosen, "dp", axis=0, tiled=True)


def solution(mesh):
    return jax.shard_map(
        body,
        mesh=mesh,
        in_specs=(
            P("dp", None, "shard", None),
            P(),
            P(),
            P(("dp", "shard"), None, None),
            P(("dp", "shard"), None, None),
        ),
        out_specs=P(None, "shard", None),
        check_vma=False,
    )
```

profile of v0, /device:TPU:0, one launch (start us, length us, event | category | flops | bytes accessed | tf_op | source)
XLA Modules:
  0.0 82.9 jit_solution(6989962412741322813)
XLA Ops:
  6.5 0.7 reduce-scatter.2.cloned.1.call-update
  7.3 0.7 copy-done.3
  8.1 0.1 copy.34
  8.3 0.1 reshape.160
  8.4 0.7 copy-done.2
  9.1 0.6 gather_fusion
  9.8 0.1 copy.33
  9.9 0.2 select_reduce_fusion
  10.1 21.9 %reduce-scatter.2.cloned.1.call-done = bf16[4,32,256]{2,1,0:T(8,128)(2,1)} async-done(((bf16[16,32,256]{2,1,0:T(8,128)(2,1)}), bf16[4,32,256]{2,1,0:T(8,128)(2,1)}) %reduce-scatter.2.cloned.1.call-update) | async-done | bytes 65552 | tf_op jit(solution)/shard_map/reduce_scatter | solution.py:68
  31.9 1.4 %gather_fusion.1 = bf16[16,32,256]{2,1,0:T(8,128)(2,1)S(1)} fusion(bf16[4,32,256]{2,1,0:T(8,128)(2,1)} %reduce-scatter.2.cloned.1.call-done, s32[1024]{0:T(1024)S(1)} %pad_clamp_fusion.1), kind=kCustom, calls=%fused_computation.1 | custom fusion | bytes 524352 | tf_op jit(solution)/shard_map/jit(_take)/gather | solution.py:72
  33.3 0.1 broadcast_select_fusion
  33.4 0.7 copy.36
  34.2 3.9 %all-to-all-start = ((bf16[2,8,32,256]{3,2,0,1:T(8,128)(2,1)}), bf16[2,8,32,256]{3,2,0,1:T(8,128)(2,1)S(1)}, u32[]{:S(2)}, u32[]{:S(2)}) async-start(bf16[2,8,32,256]{3,2,0,1:T(8,128)(2,1)} %copy.36), calls=%async_computation.1 | async-start | bytes 524288 | tf_op jit(solution)/shard_map/all_to_all | solution.py:73
  38.1 6.9 %all-to-all-done = bf16[2,8,32,256]{3,2,0,1:T(8,128)(2,1)S(1)} async-done(((bf16[2,8,32,256]{3,2,0,1:T(8,128)(2,1)}), bf16[2,8,32,256]{3,2,0,1:T(8,128)(2,1)S(1)}, u32[]{:S(2)}, u32[]{:S(2)}) %all-to-all-start) | async-done | bytes 262176 | tf_op jit(solution)/shard_map/all_to_all | solution.py:73
  45.0 0.4 multiply_reduce_fusion.2
  45.4 0.6 copy-done.1
  46.0 0.4 multiply_reduce_fusion.3
  46.4 0.2 subtract_convert_fusion
  46.6 0.5 convolution_convert_fusion.1
  47.1 0.3 fusion.5
  47.5 0.5 convolution_convert_fusion.5
  48.0 0.3 fusion.4
  48.3 0.4 convolution_convert_fusion.3
  48.6 0.5 multiply_reduce_fusion
  49.2 0.2 multiply_reduce_fusion.1
  49.3 0.1 multiply_convert_fusion
  49.5 0.7 copy.39
  50.2 3.4 %all-to-all-start.1 = ((bf16[2,8,32,256]{3,2,0,1:T(8,128)(2,1)}), bf16[2,8,32,256]{3,2,0,1:T(8,128)(2,1)S(1)}, u32[]{:S(2)}, u32[]{:S(2)}) async-start(bf16[2,8,32,256]{3,2,0,1:T(8,128)(2,1)} %copy.39), calls=%async_computation.2 | async-start | bytes 524288 | tf_op jit(solution)/shard_map/all_to_all | solution.py:77
  53.7 6.8 %all-to-all-done.1 = bf16[2,8,32,256]{3,2,0,1:T(8,128)(2,1)S(1)} async-done(((bf16[2,8,32,256]{3,2,0,1:T(8,128)(2,1)}), bf16[2,8,32,256]{3,2,0,1:T(8,128)(2,1)S(1)}, u32[]{:S(2)}, u32[]{:S(2)}) %all-to-all-start.1) | async-done | bytes 262176 | tf_op jit(solution)/shard_map/all_to_all | solution.py:77
  60.5 0.6 gather_fusion.2
  61.1 14.2 %all_gather.3 = bf16[16,32,256]{2,1,0:T(8,128)(2,1)S(1)} all-gather(bf16[4,32,256]{2,1,0:T(8,128)(2,1)S(1)} %select_select_fusion), channel_id=1, replica_groups=mesh['dp'=4,'shard'=8] {'dp'}, dimensions={0}, use_global_device_ids=true | all-gather | bytes 327680 | tf_op jit(solution)/shard_map/all_gather | solution.py:88
  75.3 0.7 copy.43
  (29 shorter events, 0.6 us)
Async XLA Ops:
  6.5 25.4 %reduce-scatter.2.cloned.1.call-start = ((), (), s32[]{:S(2)}) async-start(), calls=%async_computation.3 | async-start | bytes 327680 | tf_op jit(solution)/shard_map/reduce_scatter | solution.py:68
  7.3 0.7 copy-start.3
  8.4 0.7 copy-start.2
  34.2 10.8 %copy-start = (f32[2,256,256]{2,1,0:T(8,128)S(1)}, f32[2,256,256]{2,1,0:T(8,128)}, u32[]{:S(2)}) copy-start(f32[2,256,256]{2,1,0:T(8,128)} %param.9) | copy-start | bytes 1572868
  34.2 10.8 %all-to-all-start = ((bf16[2,8,32,256]{3,2,0,1:T(8,128)(2,1)}), bf16[2,8,32,256]{3,2,0,1:T(8,128)(2,1)S(1)}, u32[]{:S(2)}, u32[]{:S(2)}) async-start(bf16[2,8,32,256]{3,2,0,1:T(8,128)(2,1)} %copy.36), calls=%async_computation.1 | async-start | bytes 524288 | tf_op jit(solution)/shard_map/all_to_all | solution.py:73
  45.0 1.0 %copy-start.1 = (f32[2,256,256]{2,1,0:T(8,128)S(1)}, f32[2,256,256]{2,1,0:T(8,128)}, u32[]{:S(2)}) copy-start(f32[2,256,256]{2,1,0:T(8,128)} %param.8) | copy-start | bytes 1572868
  50.2 10.3 %all-to-all-start.1 = ((bf16[2,8,32,256]{3,2,0,1:T(8,128)(2,1)}), bf16[2,8,32,256]{3,2,0,1:T(8,128)(2,1)S(1)}, u32[]{:S(2)}, u32[]{:S(2)}) async-start(bf16[2,8,32,256]{3,2,0,1:T(8,128)(2,1)} %copy.39), calls=%async_computation.2 | async-start | bytes 524288 | tf_op jit(solution)/shard_map/all_to_all | solution.py:77
Sparse Core Ops, SparseCore 0:
  9.6 22.2 reduce-scatter.1
where the time goes:
time: 83.3 us; the launch traced here: 82.9 us
  waiting for transfers between devices  36.3 us (44%)
  blocking collectives  14.2 us (17%)
  between operations  13.6 us (16%)
  starting transfers between devices  7.29 us (9%)
  local copies, waits for them, and re-layouts  7.25 us (9%)
  matrix products  3.23 us (4%)
  other arithmetic  1.01 us (1%)
    reduce_scatter x1, waiting for transfers between devices, body(): lax.psum_scatter(local_terms.astype(jnp.bfloat16), 'dp', scatter_dimensio...  21.9 us
    all_gather x1, blocking collectives, body(): return lax.all_gather(chosen, 'dp', axis=0, tiled=True)  14.2 us
    all_to_all x1, waiting for transfers between devices, body(): lax.all_to_all(outgoing, 'shard', split_axis=1, concat_axis=1, tiled=True)  6.91 us
    all_to_all x1, waiting for transfers between devices, body(): lax.all_to_all(fresh.reshape(CAP, owners, row_count, block_width), 'shard...  6.81 us
    all_to_all x1, starting transfers between devices, body(): lax.all_to_all(outgoing, 'shard', split_axis=1, concat_axis=1, tiled=True)  3.87 us
    all_to_all x1, starting transfers between devices, body(): lax.all_to_all(fresh.reshape(CAP, owners, row_count, block_width), 'shard...  3.41 us
    unnamed x10, local copies, waits for them, and re-layouts  2.79 us
  transfers between devices with their start and end apart: 3, of which 3 were waited for; matrix products, arithmetic and copies ran while one was open for 2% of the time, Pallas kernels for 0%

commit v1 on v0

--- a/solution.py
+++ b/solution.py
@@ -1,9 +1,14 @@
+import functools
+
 import jax
 import jax.numpy as jnp
 from jax import lax
+from jax.experimental import pallas as pl
+from jax.experimental.pallas import tpu as pltpu
 from jax.sharding import PartitionSpec as P
 
 CAP = 2
+MESH = pl.DeviceIdType.MESH
 
 
 stat_decay = 0.9
@@ -88,9 +93,269 @@
     return lax.all_gather(chosen, "dp", axis=0, tiled=True)
 
 
+def start_factor(factor, unit_matrix):
+    size_now = factor.shape[0]
+    mean_square = jnp.sum(factor * factor, keepdims=True) * (1.0 / (size_now * size_now))
+    inverse_scale = 1.0 / (size_now * jnp.sqrt(mean_square + eps_small))
+    start = factor * inverse_scale
+    first = (1.25 * unit_matrix - 0.25 * start).astype(jnp.bfloat16)
+    return start.astype(jnp.bfloat16), first
+
+
+def dot(a, b):
+    return jnp.dot(a, b, preferred_element_type=jnp.float32)
+
+
+def refresh_slot(grad_block, left_prev, right_prev):
+    size_now = grad_block.shape[0]
+    rows = lax.broadcasted_iota(jnp.int32, (size_now, size_now), 0)
+    cols = lax.broadcasted_iota(jnp.int32, (size_now, size_now), 1)
+    unit_matrix = jnp.where(rows == cols, 1.0, 0.0).astype(jnp.float32)
+    gram_left = lax.dot_general(
+        grad_block, grad_block, (((1,), (1,)), ((), ())), preferred_element_type=jnp.float32
+    )
+    gram_right = lax.dot_general(
+        grad_block, grad_block, (((0,), (0,)), ((), ())), preferred_element_type=jnp.float32
+    )
+    factors = (
+        stat_decay * left_prev + (1.0 - stat_decay) * gram_left,
+        stat_decay * right_prev + (1.0 - stat_decay) * gram_right,
+    )
+    pairs = [start_factor(factor, unit_matrix) for factor in factors]
+    squares = [dot(first, first).astype(jnp.bfloat16) for _, first in pairs]
+    fourths = [dot(square, square).astype(jnp.bfloat16) for square in squares]
+    states = [dot(fourth, start) for fourth, (start, _) in zip(fourths, pairs)]
+    seconds = [(1.25 * unit_matrix - 0.25 * state).astype(jnp.bfloat16) for state in states]
+    roots = [
+        dot(first, second).astype(jnp.bfloat16) for (_, first), second in zip(pairs, seconds)
+    ]
+    half_done = dot(roots[0], grad_block).astype(jnp.bfloat16)
+    precond = dot(half_done, roots[1])
+    grad_wide = grad_block.astype(jnp.float32)
+    share = 1.0 / (size_now * size_now)
+    grad_norm = jnp.sqrt(jnp.sum(grad_wide * grad_wide, keepdims=True) * share + eps_small)
+    cond_norm = jnp.sqrt(jnp.sum(precond * precond, keepdims=True) * share + eps_small)
+    return (precond * (grad_norm / cond_norm)).astype(jnp.bfloat16)
+
+
+def kernel(
+    groups,
+    owners,
+    table_ref,
+    counts_ref,
+    grads_ref,
+    left_ref,
+    right_ref,
+    out_ref,
+    own_terms,
+    terms,
+    summed,
+    outgoing,
+    arrived,
+    left_held,
+    right_held,
+    fresh,
+    returned,
+    chosen,
+    local_sems,
+    sum_send,
+    sum_recv,
+    go_send,
+    go_recv,
+    back_send,
+    back_recv,
+    last_send,
+    last_recv,
+):
+    my_group = lax.axis_index("dp")
+    me = lax.axis_index("shard")
+    per_group, row_count, _ = own_terms.shape
+    slot_total = owners * CAP
+
+    def group_at(step):
+        return lax.rem(my_group + step, groups)
+
+    def owner_at(step):
+        return lax.rem(me + step, owners)
+
+    def group_blocks(group):
+        return pl.ds(group * per_group, per_group)
+
+    def rows_of(owner):
+        return pl.ds(pl.multiple_of(owner * row_count, row_count), row_count)
+
+    own_copy = pltpu.make_async_copy(
+        grads_ref.at[0, group_blocks(my_group)], own_terms, local_sems.at[0]
+    )
+    own_copy.start()
+    held_copies = []
+    for slot in range(CAP):
+        for side, (source, held) in enumerate(((left_ref, left_held), (right_ref, right_held))):
+            copy = pltpu.make_async_copy(
+                source.at[slot], held.at[slot], local_sems.at[2 + slot * 2 + side]
+            )
+            copy.start()
+            held_copies.append(copy)
+
+    barrier = pltpu.get_barrier_semaphore()
+    for step in range(1, groups):
+        pl.semaphore_signal(
+            barrier, inc=1, device_id=(group_at(step), me), device_id_type=MESH
+        )
+    for step in range(1, owners):
+        pl.semaphore_signal(
+            barrier, inc=1, device_id=(my_group, owner_at(step)), device_id_type=MESH
+        )
+    pl.semaphore_wait(barrier, groups + owners - 2)
+
+    sum_copies = []
+    for step in range(1, groups):
+        copy = pltpu.make_async_remote_copy(
+            src_ref=grads_ref.at[0, group_blocks(group_at(step))],
+            dst_ref=terms.at[step - 1],
+            send_sem=sum_send.at[step - 1],
+            recv_sem=sum_recv.at[step - 1],
+            device_id=(group_at(step), me),
+            device_id_type=MESH,
+        )
+        copy.start()
+        sum_copies.append(copy)
+
+    picks = [jnp.int32(slot_total)] * per_group
+    for slot in reversed(range(slot_total)):
+        live = slot % CAP < counts_ref[my_group, slot // CAP]
+        named = jnp.where(live, table_ref[my_group, slot], -1)
+        picks = [jnp.where(named == block, slot, pick) for block, pick in enumerate(picks)]
+
+    own_copy.wait()
+    for copy in sum_copies:
+        copy.wait_recv()
+    total = own_terms[...].astype(jnp.float32)
+    for step in range(groups - 1):
+        total += terms[step].astype(jnp.float32)
+    summed[...] = total.astype(jnp.bfloat16)
+
+    go_copies = []
+    for slot in range(CAP):
+        slot_copies = []
+        for step in range(1, owners):
+            owner = owner_at(step)
+            place = slot * owners + step
+            outgoing[place] = summed[table_ref[my_group, owner * CAP + slot]]
+            copy = pltpu.make_async_remote_copy(
+                src_ref=outgoing.at[place],
+                dst_ref=arrived.at[slot, rows_of(me)],
+                send_sem=go_send.at[place],
+                recv_sem=go_recv.at[place],
+                device_id=(my_group, owner),
+                device_id_type=MESH,
+            )
+            copy.start()
+            slot_copies.append(copy)
+        arrived[slot, rows_of(me)] = summed[table_ref[my_group, me * CAP + slot]]
+        go_copies.append(slot_copies)
+
+    back_copies = []
+    for slot in range(CAP):
+        for copy in held_copies[2 * slot : 2 * slot + 2] :
+            copy.wait()
+        for copy in go_copies[slot]:
+            copy.wait_recv()
+        fresh[slot] = refresh_slot(arrived[slot], left_held[slot], right_held[slot])
+        for step in range(1, owners):
+            owner = owner_at(step)
+            place = slot * owners + step
+            copy = pltpu.make_async_remote_copy(
+                src_ref=fresh.at[slot, rows_of(owner)],
+                dst_ref=returned.at[me * CAP + slot],
+                send_sem=back_send.at[place],
+                recv_sem=back_recv.at[place],
+                device_id=(my_group, owner),
+                device_id_type=MESH,
+            )
+            copy.start()
+            back_copies.append(copy)
+        returned[me * CAP + slot] = fresh[slot, rows_of(me)]
+
+    for copy in back_copies:
+        copy.wait_recv()
+    for block, pick in enumerate(picks):
+        keep = jnp.where(pick < slot_total, 1.0, 0.0).astype(jnp.float32)
+        picked = returned[jnp.minimum(pick, slot_total - 1)]
+        chosen[block] = (picked.astype(jnp.float32) * keep).astype(jnp.bfloat16)
+
+    last_copies = []
+    for step in range(1, groups):
+        copy = pltpu.make_async_remote_copy(
+            src_ref=chosen,
+            dst_ref=out_ref.at[group_blocks(my_group)],
+            send_sem=last_send.at[step - 1],
+            recv_sem=last_recv.at[step - 1],
+            device_id=(group_at(step), me),
+            device_id_type=MESH,
+        )
+        copy.start()
+        last_copies.append(copy)
+    out_copy = pltpu.make_async_copy(
+        chosen, out_ref.at[group_blocks(my_group)], local_sems.at[1]
+    )
+    out_copy.start()
+    for copy in sum_copies + go_copies[0] + go_copies[1] + back_copies:
+        copy.wait_send()
+    out_copy.wait()
+    for copy in last_copies:
+        copy.wait()
+
+
+def fused_body(grads, owner_table, block_counts, prev_left, prev_right):
+    owners = lax.axis_size("shard")
+    groups = lax.axis_size("dp")
+    _, blocks, row_count, width = grads.shape
+    per_group = blocks // groups
+    dma = pltpu.SemaphoreType.DMA
+    part = (per_group, row_count, width)
+    return pl.pallas_call(
+        functools.partial(kernel, groups, owners),
+        out_shape=jax.ShapeDtypeStruct((blocks, row_count, width), jnp.bfloat16),
+        in_specs=[pl.BlockSpec(memory_space=pltpu.SMEM)] * 2
+        + [pl.BlockSpec(memory_space=pl.ANY)] * 3,
+        out_specs=pl.BlockSpec(memory_space=pl.ANY),
+        scratch_shapes=[
+            pltpu.VMEM(part, jnp.bfloat16),
+            pltpu.VMEM((groups - 1,) + part, jnp.bfloat16),
+            pltpu.VMEM(part, jnp.bfloat16),
+            pltpu.VMEM((CAP * owners, row_count, width), jnp.bfloat16),
+            pltpu.VMEM((CAP, width, width), jnp.bfloat16),
+            pltpu.VMEM((CAP, width, width), jnp.float32),
+            pltpu.VMEM((CAP, width, width), jnp.float32),
+            pltpu.VMEM((CAP, width, width), jnp.bfloat16),
+            pltpu.VMEM((CAP * owners, row_count, width), jnp.bfloat16),
+            pltpu.VMEM(part, jnp.bfloat16),
+            dma((2 + 2 * CAP,)),
+            dma((groups - 1,)),
+            dma((groups - 1,)),
+            dma((CAP * owners,)),
+            dma((CAP * owners,)),
+            dma((CAP * owners,)),
+            dma((CAP * owners,)),
+            dma((groups - 1,)),
+            dma((groups - 1,)),
+        ],
+        compiler_params=pltpu.CompilerParams(
+            collective_id=0, has_side_effects=True, vmem_limit_bytes=48 * 1024 * 1024
+        ),
+    )(owner_table, block_counts, grads, prev_left, prev_right)
+
+
+def either_body(grads, *others):
+    if grads.shape[2] % 16:
+        return body(grads, *others)
+    return fused_body(grads, *others)
+
+
 def solution(mesh):
     return jax.shard_map(
-        body,
+        either_body,
         mesh=mesh,
         in_specs=(
             P("dp", None, "shard", None),

time: 83.3 us -> 36.4 us (0.44)
  waiting for transfers between devices: 36.3 us -> 0 us
  Pallas kernels: 0 us -> 31 us
  blocking collectives: 14.2 us -> 0 us
  between operations: 13.6 us -> 0.01 us
  starting transfers between devices: 7.29 us -> 0 us
  matrix products: 3.23 us -> 0 us
  local copies, waits for them, and re-layouts: 7.25 us -> 5.1 us
  other arithmetic: 1.01 us -> 0 us
    pallas_call x0 -> x1, Pallas kernels: none -> 31 us  [fused_body(): pl.pallas_call(functools.partial(kernel, groups, owners), out_shape=jax.S...]
    reduce_scatter x1 -> x0, waiting for transfers between devices: 21.9 us -> none  [body(): lax.psum_scatter(local_terms.astype(jnp.bfloat16), 'dp', scatter_dimensio...]
    all_gather x1 -> x0, blocking collectives: 14.2 us -> none  [body(): return lax.all_gather(chosen, 'dp', axis=0, tiled=True)]
    all_to_all x2 -> x0, waiting for transfers between devices: 13.7 us -> none  [the longest x1 6.91 us: body(): lax.all_to_all(outgoing, 'shard', split_axis=1, concat_axis=1, tiled=True)]
    all_to_all x2 -> x0, starting transfers between devices: 7.29 us -> none  [the longest x1 3.87 us: body(): lax.all_to_all(outgoing, 'shard', split_axis=1, concat_axis=1, tiled=True)]
    dot_general x8 -> x0, matrix products: 3.23 us -> none  [the longest x2 0.99 us: inverse_root(): jnp.dot(square, square, preferred_element_type=jnp.float32)]
    gather x3 -> x0, local copies, waits for them, and re-layouts: 2.51 us -> none  [the longest x1 1.4 us: body(): outgoing = jnp.take(summed, table_row, axis=0)]
    unnamed x10 -> x11, local copies, waits for them, and re-layouts: 2.79 us -> 5.1 us
  transfers between devices with their start and end apart: 3 -> 0, of which waited for: 3 -> 0; matrix products, arithmetic and copies ran while one was open for 2% -> 0% of each run, Pallas kernels for 0% -> 0%
where the time goes in v1:
time: 36.4 us; the launch traced here: 36.1 us
  Pallas kernels  31 us (85%)
  local copies, waits for them, and re-layouts  5.1 us (14%)
    pallas_call x1, Pallas kernels, fused_body(): pl.pallas_call(functools.partial(kernel, groups, owners), out_shape=jax.S...  31 us
    unnamed x11, local copies, waits for them, and re-layouts  5.1 us

profile of v1, /device:TPU:0, one launch (start us, length us, event | category | flops | bytes accessed | tf_op | source)
XLA Modules:
  0.0 36.1 jit_solution(14436461310882149190)
XLA Ops:
  0.0 0.0 copy-start
  0.0 1.0 %copy-done = f32[2,256,256]{2,1,0:T(8,128)S(1)} copy-done((f32[2,256,256]{2,1,0:T(8,128)S(1)}, f32[2,256,256]{2,1,0:T(8,128)}, u32[]{:S(2)}) %copy-start) | copy-done | bytes 524312
  1.0 0.0 copy-start.1
  1.0 1.0 %copy-done.1 = f32[2,256,256]{2,1,0:T(8,128)S(1)} copy-done((f32[2,256,256]{2,1,0:T(8,128)S(1)}, f32[2,256,256]{2,1,0:T(8,128)}, u32[]{:S(2)}) %copy-start.1) | copy-done | bytes 524312
  2.1 0.0 copy-start.2
  2.1 0.9 %copy-done.2 = bf16[1,16,32,256]{3,2,1,0:T(8,128)(2,1)S(1)} copy-done((bf16[1,16,32,256]{3,2,1,0:T(8,128)(2,1)S(1)}, bf16[1,16,32,256]{3,2,1,0:T(8,128)(2,1)}, u32[]{:S(2)}) %copy-start.2) | copy-done | bytes 262168
  3.0 0.0 copy-start.3
  3.0 0.7 %copy-done.3 = s32[4,16]{1,0:T(4,128)S(1)} copy-done((s32[4,16]{1,0:T(4,128)S(1)}, s32[4,16]{1,0:T(4,128)}, u32[]{:S(2)}) %copy-start.3) | copy-done | bytes 280
  3.7 0.0 copy-start.4
  3.7 0.7 %copy-done.4 = s32[4,8]{1,0:T(4,128)S(1)} copy-done((s32[4,8]{1,0:T(4,128)S(1)}, s32[4,8]{1,0:T(4,128)}, u32[]{:S(2)}) %copy-start.4) | copy-done | bytes 152
  4.4 31.0 %shard_map.55 = bf16[16,32,256]{2,1,0:T(8,128)(2,1)S(1)} custom-call(s32[4,16]{1,0:T(4,128)S(1)} %copy-done.3, s32[4,8]{1,0:T(4,128)S(1)} %copy-done.4, bf16[1,16,32,256]{3,2,1,0:T(8,128)(2,1)S(1)} %copy-done.2, f32[2,256,256]{2,1,0:T(8,128)S(1)} %copy-done, f32[2,256,256]{2,1,0:T(8,128)S(1)} %copy-done.1), custom_call_target="tpu_custom_call" | custom-call | tf_op jit(solution)/shard_map/pallas_call | solution.py:317
  35.4 0.7 %copy.7 = bf16[16,32,256]{2,1,0:T(8,128)(2,1)} copy(bf16[16,32,256]{2,1,0:T(8,128)(2,1)S(1)} %shard_map.55) | data formatting | bytes 524288
Async XLA Ops:
  0.0 1.0 %copy-start = (f32[2,256,256]{2,1,0:T(8,128)S(1)}, f32[2,256,256]{2,1,0:T(8,128)}, u32[]{:S(2)}) copy-start(f32[2,256,256]{2,1,0:T(8,128)} %left_ref.1) | copy-start | bytes 1572868
  1.0 1.0 %copy-start.1 = (f32[2,256,256]{2,1,0:T(8,128)S(1)}, f32[2,256,256]{2,1,0:T(8,128)}, u32[]{:S(2)}) copy-start(f32[2,256,256]{2,1,0:T(8,128)} %right_ref.1) | copy-start | bytes 1572868
  2.1 0.9 %copy-start.2 = (bf16[1,16,32,256]{3,2,1,0:T(8,128)(2,1)S(1)}, bf16[1,16,32,256]{3,2,1,0:T(8,128)(2,1)}, u32[]{:S(2)}) copy-start(bf16[1,16,32,256]{3,2,1,0:T(8,128)(2,1)} %grads_ref.1) | copy-start | bytes 786436
  3.0 0.7 %copy-start.3 = (s32[4,16]{1,0:T(4,128)S(1)}, s32[4,16]{1,0:T(4,128)}, u32[]{:S(2)}) copy-start(s32[4,16]{1,0:T(4,128)} %table_ref.1) | copy-start | bytes 772
  3.7 0.7 %copy-start.4 = (s32[4,8]{1,0:T(4,128)S(1)}, s32[4,8]{1,0:T(4,128)}, u32[]{:S(2)}) copy-start(s32[4,8]{1,0:T(4,128)} %counts_ref.1) | copy-start | bytes 388

commit v2 on v1

--- a/solution.py
+++ b/solution.py
@@ -123,11 +123,11 @@
     )
     pairs = [start_factor(factor, unit_matrix) for factor in factors]
     squares = [dot(first, first).astype(jnp.bfloat16) for _, first in pairs]
+    products = [dot(first, start).astype(jnp.bfloat16) for start, first in pairs]
     fourths = [dot(square, square).astype(jnp.bfloat16) for square in squares]
-    states = [dot(fourth, start) for fourth, (start, _) in zip(fourths, pairs)]
-    seconds = [(1.25 * unit_matrix - 0.25 * state).astype(jnp.bfloat16) for state in states]
     roots = [
-        dot(first, second).astype(jnp.bfloat16) for (_, first), second in zip(pairs, seconds)
+        (1.25 * first.astype(jnp.float32) - 0.25 * dot(fourth, product)).astype(jnp.bfloat16)
+        for fourth, product, (_, first) in zip(fourths, products, pairs)
     ]
     half_done = dot(roots[0], grad_block).astype(jnp.bfloat16)
     precond = dot(half_done, roots[1])
@@ -138,15 +138,41 @@
     return (precond * (grad_norm / cond_norm)).astype(jnp.bfloat16)
 
 
+def rank_slots(group, step, groups, owners, table_ref, counts_ref, ranks):
+    per_group = ranks.shape[0] // groups
+    found = jnp.int32(0)
+    places = [jnp.int32(0)] * per_group
+    block_ranks = [jnp.int32(-1)] * per_group
+    for place in range(CAP * owners):
+        slot, owner = place // owners, place % owners
+        live = slot < counts_ref[group, owner]
+        named = jnp.where(live, table_ref[group, owner * CAP + slot], -1)
+        block_ranks = [
+            jnp.where(named == block, found, rank) for block, rank in enumerate(block_ranks)
+        ]
+        if step == 0:
+            open_rank = jnp.where(live, found, -1)
+            places = [
+                jnp.where(open_rank == rank, place, held) for rank, held in enumerate(places)
+            ]
+        found = found + live.astype(jnp.int32)
+    for block, rank in enumerate(block_ranks):
+        ranks[step * per_group + block] = rank
+    return places
+
+
 def kernel(
     groups,
     owners,
-    table_ref,
-    counts_ref,
+    table_hbm,
+    counts_hbm,
     grads_ref,
     left_ref,
     right_ref,
     out_ref,
+    table_ref,
+    counts_ref,
+    ranks,
     own_terms,
     terms,
     summed,
@@ -156,7 +182,8 @@
     right_held,
     fresh,
     returned,
-    chosen,
+    returned_late,
+    gathered,
     local_sems,
     sum_send,
     sum_recv,
@@ -184,6 +211,10 @@
     def rows_of(owner):
         return pl.ds(pl.multiple_of(owner * row_count, row_count), row_count)
 
+    table_copy = pltpu.make_async_copy(table_hbm, table_ref, local_sems.at[1])
+    counts_copy = pltpu.make_async_copy(counts_hbm, counts_ref, local_sems.at[2])
+    table_copy.start()
+    counts_copy.start()
     own_copy = pltpu.make_async_copy(
         grads_ref.at[0, group_blocks(my_group)], own_terms, local_sems.at[0]
     )
@@ -192,7 +223,7 @@
     for slot in range(CAP):
         for side, (source, held) in enumerate(((left_ref, left_held), (right_ref, right_held))):
             copy = pltpu.make_async_copy(
-                source.at[slot], held.at[slot], local_sems.at[2 + slot * 2 + side]
+                source.at[slot], held.at[slot], local_sems.at[3 + slot * 2 + side]
             )
             copy.start()
             held_copies.append(copy)
@@ -221,11 +252,11 @@
         copy.start()
         sum_copies.append(copy)
 
-    picks = [jnp.int32(slot_total)] * per_group
-    for slot in reversed(range(slot_total)):
-        live = slot % CAP < counts_ref[my_group, slot // CAP]
-        named = jnp.where(live, table_ref[my_group, slot], -1)
-        picks = [jnp.where(named == block, slot, pick) for block, pick in enumerate(picks)]
+    table_copy.wait()
+    counts_copy.wait()
+    places = rank_slots(group_at(0), 0, groups, owners, table_ref, counts_ref, ranks)
+    for step in range(1, groups):
+        rank_slots(group_at(groups - step), step, groups, owners, table_ref, counts_ref, ranks)
 
     own_copy.wait()
     for copy in sum_copies:
@@ -255,56 +286,68 @@
         arrived[slot, rows_of(me)] = summed[table_ref[my_group, me * CAP + slot]]
         go_copies.append(slot_copies)
 
+    early = -(-per_group // CAP)
+    parts = (range(early), range(early, per_group))
+    landing = (returned, returned_late)
     back_copies = []
+    last_copies = []
     for slot in range(CAP):
-        for copy in held_copies[2 * slot : 2 * slot + 2] :
+        for copy in held_copies[2 * slot : 2 * slot + 2]:
             copy.wait()
         for copy in go_copies[slot]:
             copy.wait_recv()
         fresh[slot] = refresh_slot(arrived[slot], left_held[slot], right_held[slot])
+        slot_copies = []
         for step in range(1, owners):
             owner = owner_at(step)
             place = slot * owners + step
             copy = pltpu.make_async_remote_copy(
                 src_ref=fresh.at[slot, rows_of(owner)],
-                dst_ref=returned.at[me * CAP + slot],
+                dst_ref=landing[slot].at[me],
                 send_sem=back_send.at[place],
                 recv_sem=back_recv.at[place],
                 device_id=(my_group, owner),
                 device_id_type=MESH,
             )
             copy.start()
-            back_copies.append(copy)
-        returned[me * CAP + slot] = fresh[slot, rows_of(me)]
-
-    for copy in back_copies:
+            slot_copies.append(copy)
+        landing[slot][me] = fresh[slot, rows_of(me)]
+        back_copies.append(slot_copies)
+
+    for slot in range(CAP):
+        for copy in back_copies[slot]:
+            copy.wait_recv()
+        for rank in parts[slot]:
+            picked = returned[jnp.minimum(places[rank], owners - 1)]
+            if slot:
+                late = returned_late[jnp.maximum(places[rank] - owners, 0)]
+                picked = lax.select(places[rank] < owners, picked, late)
+            gathered[0, rank] = picked
+        piece = pl.ds(parts[slot].start, len(parts[slot]))
+        for step in range(1, groups):
+            copy = pltpu.make_async_remote_copy(
+                src_ref=gathered.at[0, piece],
+                dst_ref=gathered.at[step, piece],
+                send_sem=last_send.at[slot * groups + step],
+                recv_sem=last_recv.at[slot * groups + step],
+                device_id=(group_at(step), me),
+                device_id_type=MESH,
+            )
+            copy.start()
+            last_copies.append(copy)
+    for copy in sum_copies + sum(go_copies, []) + sum(back_copies, []):
+        copy.wait_send()
+    for copy in last_copies:
         copy.wait_recv()
-    for block, pick in enumerate(picks):
-        keep = jnp.where(pick < slot_total, 1.0, 0.0).astype(jnp.float32)
-        picked = returned[jnp.minimum(pick, slot_total - 1)]
-        chosen[block] = (picked.astype(jnp.float32) * keep).astype(jnp.bfloat16)
-
-    last_copies = []
-    for step in range(1, groups):
-        copy = pltpu.make_async_remote_copy(
-            src_ref=chosen,
-            dst_ref=out_ref.at[group_blocks(my_group)],
-            send_sem=last_send.at[step - 1],
-            recv_sem=last_recv.at[step - 1],
-            device_id=(group_at(step), me),
-            device_id_type=MESH,
-        )
-        copy.start()
-        last_copies.append(copy)
-    out_copy = pltpu.make_async_copy(
-        chosen, out_ref.at[group_blocks(my_group)], local_sems.at[1]
-    )
-    out_copy.start()
-    for copy in sum_copies + go_copies[0] + go_copies[1] + back_copies:
+    for step in range(groups):
+        group = group_at(groups - step)
+        for block in range(per_group):
+            rank = ranks[step * per_group + block]
+            keep = jnp.where(rank >= 0, 1.0, 0.0).astype(jnp.float32)
+            picked = gathered[step, jnp.maximum(rank, 0)].astype(jnp.float32)
+            out_ref[group * per_group + block] = (picked * keep).astype(jnp.bfloat16)
+    for copy in last_copies:
         copy.wait_send()
-    out_copy.wait()
-    for copy in last_copies:
-        copy.wait()
 
 
 def fused_body(grads, owner_table, block_counts, prev_left, prev_right):
@@ -317,10 +360,12 @@
     return pl.pallas_call(
         functools.partial(kernel, groups, owners),
         out_shape=jax.ShapeDtypeStruct((blocks, row_count, width), jnp.bfloat16),
-        in_specs=[pl.BlockSpec(memory_space=pltpu.SMEM)] * 2
-        + [pl.BlockSpec(memory_space=pl.ANY)] * 3,
-        out_specs=pl.BlockSpec(memory_space=pl.ANY),
+        in_specs=[pl.BlockSpec(memory_space=pltpu.HBM)] * 5,
+        out_specs=pl.BlockSpec(memory_space=pltpu.VMEM),
         scratch_shapes=[
+            pltpu.SMEM(owner_table.shape, jnp.int32),
+            pltpu.SMEM(block_counts.shape, jnp.int32),
+            pltpu.SMEM((blocks,), jnp.int32),
             pltpu.VMEM(part, jnp.bfloat16),
             pltpu.VMEM((groups - 1,) + part, jnp.bfloat16),
             pltpu.VMEM(part, jnp.bfloat16),
@@ -329,20 +374,21 @@
             pltpu.VMEM((CAP, width, width), jnp.float32),
             pltpu.VMEM((CAP, width, width), jnp.float32),
             pltpu.VMEM((CAP, width, width), jnp.bfloat16),
-            pltpu.VMEM((CAP * owners, row_count, width), jnp.bfloat16),
-            pltpu.VMEM(part, jnp.bfloat16),
-            dma((2 + 2 * CAP,)),
+            pltpu.VMEM((owners, row_count, width), jnp.bfloat16),
+            pltpu.VMEM((owners, row_count, width), jnp.bfloat16),
+            pltpu.VMEM((groups,) + part, jnp.bfloat16),
+            dma((3 + 2 * CAP,)),
             dma((groups - 1,)),
             dma((groups - 1,)),
             dma((CAP * owners,)),
             dma((CAP * owners,)),
             dma((CAP * owners,)),
             dma((CAP * owners,)),
-            dma((groups - 1,)),
-            dma((groups - 1,)),
+            dma((CAP * groups,)),
+            dma((CAP * groups,)),
         ],
         compiler_params=pltpu.CompilerParams(
-            collective_id=0, has_side_effects=True, vmem_limit_bytes=48 * 1024 * 1024
+            collective_id=0, has_side_effects=True, vmem_limit_bytes=62 * 1024 * 1024
         ),
     )(owner_table, block_counts, grads, prev_left, prev_right)
 

time: 36.4 us -> 31.8 us (0.87)
  local copies, waits for them, and re-layouts: 5.1 us -> 1.67 us
  Pallas kernels: 31 us -> 30 us
    unnamed x11 -> x1, local copies, waits for them, and re-layouts: 5.1 us -> 1.67 us
    pallas_call x1, Pallas kernels: 31 us -> 30 us  [fused_body(): pl.pallas_call(functools.partial(kernel, groups, owners), out_shape=jax.S...]
where the time goes in v2:
time: 31.8 us; the launch traced here: 31.6 us
  Pallas kernels  30 us (94%)
  local copies, waits for them, and re-layouts  1.67 us (5%)
    pallas_call x1, Pallas kernels, fused_body(): pl.pallas_call(functools.partial(kernel, groups, owners), out_shape=jax.S...  30 us
    unnamed x1, local copies, waits for them, and re-layouts  1.67 us

profile of v2, /device:TPU:0, one launch (start us, length us, event | category | flops | bytes accessed | tf_op | source)
XLA Modules:
  0.0 31.6 jit_solution(506759722376130312)
XLA Ops:
  0.0 30.0 %shard_map.55 = bf16[16,32,256]{2,1,0:T(8,128)(2,1)} custom-call(s32[4,16]{1,0:T(4,128)} %table_hbm.1, s32[4,8]{1,0:T(4,128)} %counts_hbm.1, bf16[1,16,32,256]{3,2,1,0:T(8,128)(2,1)} %grads_ref.1, f32[2,256,256]{2,1,0:T(8,128)} %left_ref.1, f32[2,256,256]{2,1,0:T(8,128)} %right_ref.1), custom_call_target="tpu_custom_call" | custom-call | tf_op jit(solution)/shard_map/pallas_call | solution.py:360
  30.0 1.7 %copy.7 = bf16[16,32,256]{2,1,0:T(8,128)(2,1)} copy(bf16[16,32,256]{2,1,0:T(8,128)(2,1)} %shard_map.55) | data formatting | bytes 524288
